TPU v7x, 32 devices: a whole 2x2x4 slice. The times are simulated.
32 devices in a mesh: proto: 8 (over y, x, core), batch: 4 (over z).
Axes of the slice: x: 2, y: 2, z: 4, core: 2. Of those that a mesh axis runs over, the one named last changes fastest.
Arguments:
- student_patches: bfloat16 [5120, 256], P('batch'), may hold values from -0.5 to 0.5
- teacher_patches: bfloat16 [5120, 256], P('batch'), may hold values from -0.5 to 0.5
- positions: int32 [2560], P('batch'), may hold values from 0 to 5119, as said below
- token_weight: float32 [2560], P('batch'), may hold values from 4 to 32
- student_protos: bfloat16 [16384, 256], P('proto'), may hold values from -0.1 to 0.1
- teacher_protos: bfloat16 [16384, 256], P('proto'), may hold values from -0.5 to 0.5
Outputs:
- patch_grad: bfloat16 [5120, 256], P('batch')
- proto_grad: bfloat16 [16384, 256], P('proto')
Inputs may be any that keep to these rules, and one draw needn't show every extreme that they name: `positions`: the j-th block of 640 entries holds 640 different indices among patches j * 1280 to (j + 1) * 1280 - 1; the first and last patch of each such block are always among them.
All inputs are finite; a program needn't handle non-finite values.
Results may differ from a plain program's by a relative error of at most 0.001.
The roundings to bfloat16 on the way count: a program that leaves them out, or rounds other values in their place, can miss the bound.
Values may be sent and summed in bfloat16 or wider, within the bound.
A program may use at most 64 MiB of HBM per device.

v0:
```python
import jax
import jax.numpy as jnp
from jax import lax
from jax.sharding import PartitionSpec as P

ITERS = 3


TEMP_TEACHER = 0.07
TEMP_STUDENT = 0.1
LENGTH_FLOOR = 1e-12


def unit_rows(transport_plan):
    values = transport_plan.astype(jnp.float32)
    row_norms = jnp.sqrt(jnp.sum(values * values, axis=1, keepdims=True) + LENGTH_FLOOR)
    return (values / row_norms, row_norms)


def column_scale(row_scale, teacher_assignments):
    column_sum = lax.psum(jnp.sum(row_scale[:, None] * teacher_assignments, axis=0), "batch")
    return 1.0 / column_sum


def exponentiated_similarity(front_segment, rear_segment, sharpening_divisor):
    similarity_matrix = lax.dot_general(
        front_segment, rear_segment, (((1,), (1,)), ((), ())), preferred_element_type=jnp.float32
    )
    return jnp.exp(similarity_matrix / sharpening_divisor)


def body(student_patches, teacher_patches, positions, token_weight, student_protos, teacher_protos):
    patch_count = student_patches.shape[0]
    token_count = positions.shape[0]
    local_rows = positions - lax.axis_index("batch") * patch_count
    student_unit, student_norm = unit_rows(jnp.take(student_patches, local_rows, axis=0))
    teacher_unit, unused_norm = unit_rows(jnp.take(teacher_patches, local_rows, axis=0))
    student_half = student_unit.astype(jnp.bfloat16)
    teacher_half = teacher_unit.astype(jnp.bfloat16)
    proto_unit, proto_norm = unit_rows(student_protos)
    proto_half = proto_unit.astype(jnp.bfloat16)
    target_unit, unused_target = unit_rows(teacher_protos)
    target_half = target_unit.astype(jnp.bfloat16)
    teacher_assignments = exponentiated_similarity(teacher_half, target_half, TEMP_TEACHER)
    student_table = exponentiated_similarity(student_half, proto_half, TEMP_STUDENT)
    student_part = jnp.sum(student_table, axis=1)
    row_scale = jnp.ones((token_count,), jnp.float32)
    student_total = lax.psum(student_part, "proto")
    first_iteration = 0
    for iteration in range(first_iteration, ITERS):
        col_scale = column_scale(row_scale, teacher_assignments)
        row_part = lax.psum(jnp.sum(teacher_assignments * col_scale[None, :], axis=1), "proto")
        row_scale = row_scale / (row_scale * row_part)
    probability = student_table / student_total[:, None]
    target = row_scale[:, None] * teacher_assignments * col_scale[None, :]
    coefficient = (token_weight[:, None] * (probability - target) / TEMP_STUDENT).astype(
        jnp.bfloat16
    )
    feature_term = jnp.dot(coefficient, proto_half, preferred_element_type=jnp.float32)
    feature_total = lax.psum(feature_term, "proto")
    inner_product = jnp.sum(feature_total * student_unit, axis=1, keepdims=True)
    feature_grad = ((feature_total - inner_product * student_unit) / student_norm).astype(
        jnp.bfloat16
    )
    patch_grad = (
        jnp.zeros((patch_count, feature_grad.shape[1]), jnp.bfloat16)
        .at[local_rows]
        .set(feature_grad)
    )
    proto_term = lax.dot_general(
        coefficient, student_half, (((0,), (0,)), ((), ())), preferred_element_type=jnp.float32
    )
    proto_total = lax.psum(proto_term, "batch")
    proto_inner = jnp.sum(proto_total * proto_unit, axis=1, keepdims=True)
    proto_grad = ((proto_total - proto_inner * proto_unit) / proto_norm).astype(jnp.bfloat16)
    return (patch_grad, proto_grad)


def solution(mesh):
    return jax.shard_map(
        body,
        mesh=mesh,
        in_specs=(
            P("batch", None),
            P("batch", None),
            P("batch"),
            P("batch"),
            P("proto", None),
            P("proto", None),
        ),
        out_specs=(P("batch", None), P("proto", None)),
        check_vma=False,
    )
```

profile of v0, /device:TPU:0, one launch (start us, length us, event | category | flops | bytes accessed | tf_op | source)
XLA Modules:
  0.0 268.9 jit_solution(4410565830706576882)
XLA Ops:
  7.2 0.0 all-reduce.4.cloned.1.call-start
  7.3 0.9 compare_and_fusion
  8.1 1.6 fusion.2
  9.7 1.6 fusion.1
  11.3 2.8 %gather_fusion = bf16[640,256]{1,0:T(8,128)(2,1)S(1)} fusion(bf16[1280,256]{1,0:T(8,128)(2,1)S(1)} %copy-done, s32[1024]{0:T(1024)S(1)} %pad_clamp_fusion), kind=kCustom, calls=%fused_computation.clone | custom fusion | bytes 657920 | tf_op jit(solution)/shard_map/jit(_take)/gather | solution.py:36
  14.1 2.8 %gather_fusion.1 = bf16[640,256]{1,0:T(8,128)(2,1)S(1)} fusion(bf16[1280,256]{1,0:T(8,128)(2,1)S(1)} %copy-done.1, s32[1024]{0:T(1024)S(1)} %pad_clamp_fusion), kind=kCustom, calls=%fused_computation.1.clone | custom fusion | bytes 657920 | tf_op jit(solution)/shard_map/jit(_take)/gather | solution.py:37
  16.9 0.4 fusion.6
  17.3 3.6 %fusion.23 = (f32[2048]{0:T(1024)S(1)}, f32[640,2048]{1,0:T(8,128)}) fusion(bf16[2048,256]{1,0:T(8,128)(2,1)S(1)} %copy-done.4, f32[2048]{0:T(1024)S(1)} %add_sqrt_fusion, f32[640]{0:T(1024)S(1)} %get-tuple-element.13, bf16[640,256]{1,0:T(8,128)(2,1)S(1)} %gather_fusion.1, pred[640]{0:T(1024)(128)(4,1)S(1)} %get-tuple-element.7), kind=kOutput, calls=%fused_computation.60 | convolution fusion | flops 675936256 | bytes 6638720 | tf_op jit(solution)/shard_map/dot_general | solution.py:26
  20.9 13.7 %psum.64 = f32[2048]{0:T(1024)S(1)} all-reduce(f32[2048]{0:T(1024)S(1)} %get-tuple-element.9), channel_id=1, replica_groups=mesh['proto'=8,'batch'=4] {'batch'}, use_global_device_ids=true, to_apply=%region_7.9 | all-reduce | flops 2048 | bytes 16384 | tf_op jit(solution)/shard_map/psum | solution.py:21
  34.6 2.9 %multiply_reduce_fusion.4 = f32[640]{0:T(1024)S(1)} fusion(f32[640,2048]{1,0:T(8,128)} %get-tuple-element.10, f32[2048]{0:T(1024)S(1)} %broadcast_divide_fusion.2), kind=kLoop, calls=%fused_computation.8 | loop fusion | flops 2620800 | bytes 5253632 | tf_op jit(solution)/shard_map/reduce_sum | solution.py:52
  37.5 11.8 %psum.65 = f32[640]{0:T(1024)S(1)} all-reduce(f32[640]{0:T(1024)S(1)} %multiply_reduce_fusion.4), channel_id=1, replica_groups=mesh['proto'=8,'batch'=4] {'proto'}, use_global_device_ids=true, to_apply=%region_9.11 | all-reduce | flops 640 | bytes 5120 | tf_op jit(solution)/shard_map/psum | solution.py:52
  49.3 2.9 %multiply_reduce_fusion.3 = f32[2048]{0:T(1024)S(1)} fusion(f32[640,2048]{1,0:T(8,128)} %get-tuple-element.10, f32[640]{0:T(1024)S(1)} %broadcast_divide_fusion.4), kind=kLoop, calls=%fused_computation.7 | loop fusion | flops 2619392 | bytes 5253632 | tf_op jit(solution)/shard_map/reduce_sum | solution.py:21
  52.2 8.5 %psum.66 = f32[2048]{0:T(1024)S(1)} all-reduce(f32[2048]{0:T(1024)S(1)} %multiply_reduce_fusion.3), channel_id=1, replica_groups=mesh['proto'=8,'batch'=4] {'batch'}, use_global_device_ids=true, to_apply=%region_11.13 | all-reduce | flops 2048 | bytes 16384 | tf_op jit(solution)/shard_map/psum | solution.py:21
  60.8 2.9 %multiply_reduce_fusion.2 = f32[640]{0:T(1024)S(1)} fusion(f32[640,2048]{1,0:T(8,128)} %get-tuple-element.10, f32[2048]{0:T(1024)S(1)} %broadcast_divide_fusion.1), kind=kLoop, calls=%fused_computation.6 | loop fusion | flops 2620800 | bytes 5253632 | tf_op jit(solution)/shard_map/reduce_sum | solution.py:52
  63.7 11.8 %psum.67 = f32[640]{0:T(1024)S(1)} all-reduce(f32[640]{0:T(1024)S(1)} %multiply_reduce_fusion.2), channel_id=1, replica_groups=mesh['proto'=8,'batch'=4] {'proto'}, use_global_device_ids=true, to_apply=%region_13.15 | all-reduce | flops 640 | bytes 5120 | tf_op jit(solution)/shard_map/psum | solution.py:52
  75.5 3.0 %multiply_reduce_fusion.1 = f32[2048]{0:T(1024)S(1)} fusion(f32[640,2048]{1,0:T(8,128)} %get-tuple-element.10, f32[640]{0:T(1024)S(1)} %broadcast_divide_fusion.3), kind=kLoop, calls=%fused_computation.5 | loop fusion | flops 2619392 | bytes 5253632 | tf_op jit(solution)/shard_map/reduce_sum | solution.py:21
  78.5 10.6 %psum.68 = f32[2048]{0:T(1024)S(1)} all-reduce(f32[2048]{0:T(1024)S(1)} %multiply_reduce_fusion.1), channel_id=1, replica_groups=mesh['proto'=8,'batch'=4] {'batch'}, use_global_device_ids=true, to_apply=%region_15.17 | all-reduce | flops 2048 | bytes 16384 | tf_op jit(solution)/shard_map/psum | solution.py:21
  89.2 2.9 %multiply_reduce_fusion = f32[640]{0:T(1024)S(1)} fusion(f32[640,2048]{1,0:T(8,128)} %get-tuple-element.10, f32[2048]{0:T(1024)S(1)} %broadcast_divide_fusion), kind=kLoop, calls=%fused_computation.4 | loop fusion | flops 2620800 | bytes 5253632 | tf_op jit(solution)/shard_map/reduce_sum | solution.py:52
  92.1 3.6 %fusion = (f32[640]{0:T(1024)S(1)}, f32[640,2048]{1,0:T(8,128)}) fusion(f32[2048]{0:T(1024)S(1)} %add_sqrt_fusion.1, bf16[2048,256]{1,0:T(8,128)(2,1)S(1)} %copy-done.2, f32[640]{0:T(1024)S(1)} %get-tuple-element.14, bf16[640,256]{1,0:T(8,128)(2,1)S(1)} %gather_fusion, pred[640]{0:T(1024)(128)(4,1)S(1)} %get-tuple-element.7), kind=kOutput, calls=%fused_computation.11 | convolution fusion | flops 675937664 | bytes 6633088 | tf_op jit(solution)/shard_map/dot_general | solution.py:26
  95.7 12.0 %all-reduce = (f32[640]{0:T(1024)S(1)}, f32[640]{0:T(1024)S(1)}) all-reduce(f32[640]{0:T(1024)S(1)} %multiply_reduce_fusion, f32[640]{0:T(1024)S(1)} %get-tuple-element.11), channel_id=1, replica_groups=mesh['proto'=8,'batch'=4] {'proto'}, use_global_device_ids=true, to_apply=%region_17.19 | all-reduce | flops 1280 | bytes 10240 | tf_op jit(solution)/shard_map/psum | solution.py:52
  107.8 5.0 %multiply_convert_fusion = bf16[640,2048]{1,0:T(8,128)(2,1)S(1)} fusion(f32[640,2048]{1,0:T(8,128)} %get-tuple-element.10, f32[640,2048]{1,0:T(8,128)} %get-tuple-element.12, f32[640]{0:T(1024)S(1)} %multiply_divide_fusion, f32[2048]{0:T(1024)S(1)} %broadcast_divide_fusion, f32[640]{0:T(1024)S(1)} %get-tuple-element.6, f32[640]{0:T(1024)S(1)} %copy-done.5), kind=kLoop, calls=%fused_computation.3 | loop fusion | flops 10485760 | bytes 13123072 | tf_op jit(solution)/shard_map/convert_element_type | solution.py:56
  112.8 1.5 copy-done.3
  114.3 1.8 fusion.9
  116.1 0.0 all-reduce.4.cloned.1.call-update
  116.1 0.2 all-reduce.6.cloned.1.call-start
  116.4 4.3 %fusion.19 = f32[2048,256]{1,0:T(8,128)} fusion(bf16[640,2048]{1,0:T(8,128)(2,1)} %copy-done.3, f32[640]{0:T(1024)S(1)} %get-tuple-element.14, bf16[640,256]{1,0:T(8,128)(2,1)S(1)} %gather_fusion, pred[640]{0:T(1024)(128)(4,1)S(1)} %get-tuple-element.7), kind=kOutput, calls=%fused_computation.42 | convolution fusion | flops 671744000 | bytes 5049472 | tf_op jit(solution)/shard_map/dot_general | solution.py:70
  120.7 48.1 %all-reduce.4.cloned.1.call-done = f32[640,256]{1,0:T(8,128)} async-done(((f32[640,256]{1,0:T(8,128)}), f32[640,256]{1,0:T(8,128)}) %all-reduce.4.cloned.1.call-update) | async-done | bytes 655376 | tf_op jit(solution)/shard_map/psum | solution.py:60
  168.8 1.4 multiply_reduce_fusion.6
  170.2 7.9 %scatter_custom_fusion = bf16[1280,256]{1,0:T(8,128)(2,1)} fusion(s32[640]{0:T(1024)S(1)} %get-tuple-element.8, f32[640,256]{1,0:T(8,128)} %all-reduce.4.cloned.1.call-done, f32[640]{0:T(1024)S(1)} %multiply_reduce_fusion.6, f32[640]{0:T(1024)S(1)} %get-tuple-element.14, bf16[]{:T(256)} %constant.17.clone.1, bf16[640,256]{1,0:T(8,128)(2,1)S(1)} %gather_fusion, ...), kind=kCustom, calls=%fused_computation.35 | custom fusion | flops 1146880 | bytes 1647618 | tf_op jit(solution)/shard_map/scatter | solution.py:68
  178.1 79.0 %all-reduce.6.cloned.1.call-done = f32[2048,256]{1,0:T(8,128)} async-done(((f32[2048,256]{1,0:T(8,128)}), f32[2048,256]{1,0:T(8,128)}) %all-reduce.6.cloned.1.call-update) | async-done | bytes 2097168 | tf_op jit(solution)/shard_map/psum | solution.py:73
  257.1 2.3 multiply_reduce_fusion.5
  259.3 2.7 %divide_convert_fusion = bf16[2048,256]{1,0:T(8,128)(2,1)} fusion(f32[2048,256]{1,0:T(8,128)} %all-reduce.6.cloned.1.call-done, f32[2048]{0:T(1024)S(1)} %multiply_reduce_fusion.5, f32[2048]{0:T(1024)S(1)} %add_sqrt_fusion.1, bf16[2048,256]{1,0:T(8,128)(2,1)S(1)} %copy-done.2), kind=kLoop, calls=%fused_computation.19 | loop fusion | flops 3145728 | bytes 4210688 | tf_op jit(solution)/shard_map/convert_element_type | solution.py:75
  (22 shorter events, 0.1 us)
Async XLA Ops:
  7.2 4.1 %copy-start = (bf16[1280,256]{1,0:T(8,128)(2,1)S(1)}, bf16[1280,256]{1,0:T(8,128)(2,1)}, u32[]{:S(2)}) copy-start(bf16[1280,256]{1,0:T(8,128)(2,1)} %param.8) | copy-start | bytes 1966084
  7.2 10.1 %copy-start.4 = (bf16[2048,256]{1,0:T(8,128)(2,1)S(1)}, bf16[2048,256]{1,0:T(8,128)(2,1)}, u32[]{:S(2)}) copy-start(bf16[2048,256]{1,0:T(8,128)(2,1)} %param.13) | copy-start | bytes 3145732
  7.2 6.9 %copy-start.1 = (bf16[1280,256]{1,0:T(8,128)(2,1)S(1)}, bf16[1280,256]{1,0:T(8,128)(2,1)}, u32[]{:S(2)}) copy-start(bf16[1280,256]{1,0:T(8,128)(2,1)} %param.9) | copy-start | bytes 1966084
  7.2 161.6 %all-reduce.4.cloned.1.call-start = ((), (), s32[]{:S(2)}) async-start(), calls=%async_computation | async-start | bytes 1310720 | tf_op jit(solution)/shard_map/psum | solution.py:60
  75.5 16.6 %copy-start.2 = (bf16[2048,256]{1,0:T(8,128)(2,1)S(1)}, bf16[2048,256]{1,0:T(8,128)(2,1)}, u32[]{:S(2)}) copy-start(bf16[2048,256]{1,0:T(8,128)(2,1)} %param.12) | copy-start | bytes 3145732
  92.1 15.7 %copy-start.5 = (f32[640]{0:T(1024)S(1)}, f32[640]{0:T(1024)}, u32[]{:S(2)}) copy-start(f32[640]{0:T(1024)} %param.11) | copy-start | bytes 7684
  112.8 1.5 copy-start.3
  116.1 140.9 %all-reduce.6.cloned.1.call-start = ((), (), s32[]{:S(2)}) async-start(), calls=%async_computation.1 | async-start | bytes 4194304 | tf_op jit(solution)/shard_map/psum | solution.py:73
Sparse Core Ops, SparseCore 0:
  116.3 52.4 all-reduce.3
  171.2 85.7 all-reduce.5
where the time goes:
time: 270 us; the launch traced here: 269 us
  waiting for transfers between devices  127 us (47%)
  blocking collectives  68.5 us (25%)
  other arithmetic  38.5 us (14%)
  between operations  14.3 us (5%)
  matrix products  13.3 us (5%)
  local copies, waits for them, and re-layouts  7.07 us (3%)
    psum x1, waiting for transfers between devices, body(): proto_total = lax.psum(proto_term, 'batch')  79 us
    psum x1, waiting for transfers between devices, body(): feature_total = lax.psum(feature_term, 'proto')  48.1 us
    psum x3, blocking collectives, body(): lax.psum(jnp.sum(teacher_assignments * col_scale[None, :], axis=1), 'proto')  35.6 us
    psum x3, blocking collectives, column_scale(): lax.psum(jnp.sum(row_scale[:, None] * teacher_assignments, axis=0), 'batch')  32.8 us
    reduce_sum x3, other arithmetic, body(): jnp.sum(teacher_assignments * col_scale[None, :], axis=1)  8.73 us
    scatter x1, other arithmetic, body(): patch_grad = jnp.zeros((patch_count, feature_grad.shape[1]), jnp.bfloat16...  7.9 us
    dot_general x2, matrix products, exponentiated_similarity(): lax.dot_general(front_segment, rear_segment, (((1,), (1,)), ((), ())), pr...  7.17 us
    reduce_sum x2, other arithmetic, column_scale(): jnp.sum(row_scale[:, None] * teacher_assignments, axis=0)  5.9 us
  transfers between devices with their start and end apart: 2, of which 2 were waited for; matrix products, arithmetic and copies ran while one was open for 5% of the time, Pallas kernels for 0%

commit v1 on v0

v1 whole, which is shorter than its diff:
```python
import functools
import math

import jax
import jax.numpy as jnp
from jax import lax
from jax.experimental import pallas as pl
from jax.experimental.pallas import tpu as pltpu
from jax.sharding import PartitionSpec as P

ITERS = 3
TEMP_TEACHER = 0.07
TEMP_STUDENT = 0.1
LENGTH_FLOOR = 1e-12
LOG2E = math.log2(math.e)
TEACHER_RATE = LOG2E / TEMP_TEACHER
STUDENT_RATE = LOG2E / TEMP_STUDENT
GROUP = 8
TILE = 256
LANES = 128
MESH = pl.DeviceIdType.MESH
F32 = jnp.float32
BF16 = jnp.bfloat16


def dot_nt(a, b):
    return lax.dot_general(a, b, (((1,), (1,)), ((), ())), preferred_element_type=F32)


def dot_nn(a, b):
    return jnp.dot(a, b, preferred_element_type=F32)


def row_norm(values):
    return jnp.sqrt(jnp.sum(values * values, axis=1, keepdims=True) + LENGTH_FLOOR)


def as_columns(row):
    return jnp.transpose(jnp.broadcast_to(row, (LANES, row.shape[1])))


def kernel(
    n_p, n_z,
    sp, tp, pos, weight, pp, qp,
    patch_out, proto_out,
    hot, tok, s_unit, s_norm, ph, qh, e_ref, s_ref, acc_ref, acc2_ref,
    rb_ref, ab_ref, cb_ref, crow_ref,
    row_buf, col_buf, fac_buf, feat, rs_buf, rs2_buf, fgrad,
    row_send, row_recv, col_send, col_recv, fac_send, fac_recv,
    t1_send, t1_recv, t2_send, t2_recv, t3_send, t3_recv,
    rs_send, rs_recv, rs2_send, rs2_recv, ag_send, ag_recv,
):
    tokens = tok.shape[1]
    patches, dim = sp.shape
    protos = pp.shape[0]
    share = tokens // GROUP
    octets = n_p // GROUP
    me_p = lax.axis_index("proto")
    me_z = lax.axis_index("batch")
    octet = me_p // GROUP
    g = me_p % GROUP

    def rows_of(member):
        return pl.multiple_of(((member % 2) * (GROUP // 2) + member // 2) * share, 16)

    barrier = pltpu.get_barrier_semaphore()
    for j in range(1, n_p):
        pl.semaphore_signal(barrier, inc=1, device_id=((me_p + j) % n_p, me_z), device_id_type=MESH)
    for j in range(1, n_z):
        pl.semaphore_signal(barrier, inc=1, device_id=(me_p, (me_z + j) % n_z), device_id_type=MESH)

    def remote(src, dst, send, recv, p, z):
        return pltpu.make_async_remote_copy(
            src_ref=src, dst_ref=dst, send_sem=send, recv_sem=recv,
            device_id=(p, z), device_id_type=MESH,
        )

    def row_copies(it):
        mine = row_buf.at[it, me_p]
        return [
            remote(mine, mine, row_send.at[it, j - 1], row_recv.at[it, j - 1], (me_p + j) % n_p, me_z)
            for j in range(1, n_p)
        ]

    def col_copies(it):
        mine = col_buf.at[it, me_z]
        return [
            remote(mine, mine, col_send.at[it, j - 1], col_recv.at[it, j - 1], me_p, (me_z + j) % n_z)
            for j in range(1, n_z)
        ]

    def start(copies):
        for copy in copies:
            copy.start()

    def wait(copies):
        for copy in copies:
            copy.wait()

    local = pos[...] - me_z * patches
    local_col = as_columns(local.astype(F32))
    lane = lax.broadcasted_iota(jnp.int32, (tokens, LANES), 1).astype(F32)
    for t in range(patches // LANES):
        hot[:, t * LANES:(t + 1) * LANES] = jnp.where(
            local_col == lane + float(t * LANES), 1.0, 0.0
        ).astype(BF16)

    @pl.loop(0, tokens // LANES)
    def _(i):
        rows = pl.ds(pl.multiple_of(i * LANES, LANES), LANES)
        picked = hot[rows, :]
        student = dot_nn(picked, sp[...])
        norm = row_norm(student)
        unit = student / norm
        s_unit[rows, :] = unit
        s_norm[rows, :] = jnp.broadcast_to(norm, (LANES, LANES))
        teacher = dot_nn(picked, tp[...])
        tok[me_z, rows, 0:dim] = unit.astype(BF16)
        tok[me_z, rows, dim:2 * dim] = (teacher / row_norm(teacher)).astype(BF16)

    @pl.loop(0, protos // TILE)
    def _(i):
        rows = pl.ds(pl.multiple_of(i * TILE, TILE), TILE)
        values = qp[rows, :].astype(F32)
        half = (values / row_norm(values)).astype(BF16)
        qh[rows, :] = half
        exps = jnp.exp2(dot_nt(tok[me_z, :, dim:2 * dim], half) * TEACHER_RATE)
        e_ref[:, rows] = exps
        col_buf[0, me_z, :, rows] = jnp.sum(exps, axis=0, keepdims=True)

    pl.semaphore_wait(barrier, n_p + n_z - 2)
    copies = col_copies(0)
    start(copies)

    acc2_ref[...] = jnp.zeros_like(acc2_ref)

    @pl.loop(0, protos // TILE)
    def _(i):
        rows = pl.ds(pl.multiple_of(i * TILE, TILE), TILE)
        values = pp[rows, :].astype(F32)
        half = (values / row_norm(values)).astype(BF16)
        ph[rows, :] = half
        exps = jnp.exp2(dot_nt(tok[me_z, :, 0:dim], half) * STUDENT_RATE)
        s_ref[:, rows] = exps
        acc2_ref[...] += exps[:, 0:LANES] + exps[:, LANES:2 * LANES]

    def lane_sums(ref):
        return jnp.sum(jnp.transpose(ref[...]), axis=0, keepdims=True)

    t1 = []
    for j in range(1, n_z):
        block = tok.at[me_z, pl.ds(rows_of(g), share), :]
        t1.append(remote(block, block, t1_send.at[j - 1], t1_recv.at[j - 1], me_p, (me_z + j) % n_z))
    t2 = []
    t3 = []
    other = me_p + 1 - 2 * (me_p % 2)
    for j in range(1, n_z):
        source = (me_z + n_z - j) % n_z
        block = tok.at[source, pl.ds(rows_of(g), share), :]
        for k in range(1, GROUP // 2):
            t2.append(remote(
                block, block, t2_send.at[j - 1, k - 1], t2_recv.at[j - 1, k - 1],
                octet * GROUP + (g + 2 * k) % GROUP, me_z,
            ))
        half_rows = pl.ds(pl.multiple_of((g % 2) * (tokens // 2), 16), tokens // 2)
        block = tok.at[source, half_rows, :]
        t3.append(remote(block, block, t3_send.at[j - 1], t3_recv.at[j - 1], other, me_z))

    row_scale = jnp.ones((1, tokens), F32)
    student_total = None
    for it in range(ITERS):
        if it > 0:
            def col_step(i, carry):
                rows = pl.ds(pl.multiple_of(i * 32, 32), 32)
                scale = rb_ref[rows, :]
                out = []
                for t in range(protos // LANES):
                    part = e_ref[rows, t * LANES:(t + 1) * LANES] * scale
                    out.append(carry[t] + jnp.sum(part.reshape(4, 8, LANES), axis=0))
                return tuple(out)
            sums = lax.fori_loop(
                0, tokens // 32, col_step,
                tuple(jnp.zeros((8, LANES), F32) for _ in range(protos // LANES)),
            )
            for t in range(protos // LANES):
                col_buf[it, me_z, :, t * LANES:(t + 1) * LANES] = jnp.sum(sums[t], axis=0, keepdims=True)
            copies = col_copies(it)
            start(copies)
        wait(copies)
        if it == 0:
            start(t1)
        total = col_buf[it, 0]
        for q in range(1, n_z):
            total = total + col_buf[it, q]
        crow_ref[...] = 1.0 / total

        @pl.loop(0, tokens // 64)
        def _(i):
            rows = pl.ds(pl.multiple_of(i * 64, 64), 64)
            running = e_ref[rows, 0:LANES] * crow_ref[:, 0:LANES]
            for t in range(1, protos // LANES):
                cols = slice(t * LANES, (t + 1) * LANES)
                running = running + e_ref[rows, cols] * crow_ref[:, cols]
            acc_ref[rows, :] = running

        row_buf[it, me_p, 0:1, :] = lane_sums(acc_ref)
        row_buf[it, me_p, 1:2, :] = lane_sums(acc2_ref)
        copies = row_copies(it)
        start(copies)
        if it == ITERS - 1:
            cb_ref[...] = as_columns(crow_ref[...])
        wait(copies)
        if it == 1:
            wait(t1)
            start(t2)
        total = row_buf[it, 0]
        for q in range(1, n_p):
            total = total + row_buf[it, q]
        row_scale = row_scale / (row_scale * total[0:1, :])
        student_total = total[1:2, :]
        if it < ITERS - 1:
            rb_ref[...] = as_columns(row_scale)

    gain = weight[...] / TEMP_STUDENT
    student_gain = gain / student_total
    teacher_gain = gain * row_scale
    fac_buf[me_z, 0:1, :] = student_gain
    fac_buf[me_z, 1:2, :] = teacher_gain
    mine = fac_buf.at[me_z]
    fac = [
        remote(mine, mine, fac_send.at[j - 1], fac_recv.at[j - 1], me_p, (me_z + j) % n_z)
        for j in range(1, n_z)
    ]
    start(fac)
    wait(t2)
    start(t3)

    rb_ref[...] = as_columns(teacher_gain)
    ab_ref[...] = as_columns(student_gain)

    @pl.loop(0, tokens // LANES)
    def _(i):
        rows = pl.ds(pl.multiple_of(i * LANES, LANES), LANES)
        a = ab_ref[rows, :]
        b = rb_ref[rows, :]
        parts = []
        for t in range(protos // LANES):
            cols = slice(t * LANES, (t + 1) * LANES)
            parts.append(
                (s_ref[rows, cols] * a - e_ref[rows, cols] * b * crow_ref[:, cols]).astype(BF16)
            )
        feat[rows, :] = dot_nn(jnp.concatenate(parts, axis=1), ph[...])

    rs = []
    for j in range(1, GROUP):
        to = (g + j) % GROUP
        rs.append(remote(
            feat.at[pl.ds(rows_of(to), share), :], rs_buf.at[j - 1],
            rs_send.at[j - 1], rs_recv.at[j - 1], octet * GROUP + to, me_z,
        ))
    start(rs)
    wait(fac)
    wait(t3)

    def proto_tile(i):
        rows = pl.ds(pl.multiple_of(i * TILE, TILE), TILE)
        p_half = ph[rows, :]
        q_half = qh[rows, :]
        c = jnp.concatenate([cb_ref[rows, :]] * (tokens // LANES), axis=1)

        def block(z, running):
            student = tok[z, :, 0:dim]
            prob = jnp.exp2(dot_nt(p_half, student) * STUDENT_RATE)
            target = jnp.exp2(dot_nt(q_half, tok[z, :, dim:2 * dim]) * TEACHER_RATE)
            coefficient = prob * fac_buf[z, 0:1, :] - target * fac_buf[z, 1:2, :] * c
            return running + dot_nn(coefficient.astype(BF16), student)

        total = jnp.zeros((TILE, dim), F32)
        if n_z <= 4:
            for z in range(n_z):
                total = block(z, total)
        else:
            total = lax.fori_loop(0, n_z, block, total)
        values = pp[rows, :].astype(F32)
        norm = row_norm(values)
        unit = values / norm
        inner = jnp.sum(total * unit, axis=1, keepdims=True)
        proto_out[rows, :] = ((total - inner * unit) / norm).astype(BF16)

    tiles = protos // TILE
    early = tiles - 3
    pl.loop(0, early)(proto_tile)

    wait(rs)
    own = pl.ds(rows_of(g), share)
    total = feat[own, :]
    for j in range(1, GROUP):
        total = total + rs_buf[j - 1]
    if octets > 1:
        rs2_buf[octet] = total
        mine2 = rs2_buf.at[octet]
        rs2 = [
            remote(mine2, mine2, rs2_send.at[j - 1], rs2_recv.at[j - 1],
                   ((octet + j) % octets) * GROUP + g, me_z)
            for j in range(1, octets)
        ]
        start(rs2)
        wait(rs2)
        total = rs2_buf[0]
        for q in range(1, octets):
            total = total + rs2_buf[q]
    unit = s_unit[own, :]
    inner = jnp.sum(total * unit, axis=1, keepdims=True)
    norm = jnp.concatenate([s_norm[own, :]] * (dim // LANES), axis=1)
    fgrad[own, :] = ((total - inner * unit) / norm).astype(BF16)
    piece = fgrad.at[own, :]
    ag = [
        remote(piece, piece, ag_send.at[j - 1], ag_recv.at[j - 1],
               octet * GROUP + (g + j) % GROUP, me_z)
        for j in range(1, GROUP)
    ]
    start(ag)

    pl.loop(early, tiles)(proto_tile)

    wait(ag)

    @pl.loop(0, patches // TILE)
    def _(i):
        rows = pl.ds(pl.multiple_of(i * TILE, TILE), TILE)
        index = lax.broadcasted_iota(jnp.int32, (TILE, tokens), 0) + i * TILE
        chosen = jnp.where(index == local, 1.0, 0.0).astype(BF16)
        patch_out[rows, :] = dot_nn(chosen, fgrad[...]).astype(BF16)


def body(n_p, n_z, sp, tp, positions, weight, pp, qp):
    patches, dim = sp.shape
    tokens = positions.shape[0]
    protos = pp.shape[0]
    share = tokens // GROUP
    octets = n_p // GROUP
    vmem = pltpu.VMEM
    dma = pltpu.SemaphoreType.DMA
    one = max(octets - 1, 1)
    scratch = [
        vmem((tokens, patches), BF16),
        vmem((n_z, tokens, 2 * dim), BF16),
        vmem((tokens, dim), F32),
        vmem((tokens, LANES), F32),
        vmem((protos, dim), BF16),
        vmem((protos, dim), BF16),
        vmem((tokens, protos), F32),
        vmem((tokens, protos), F32),
        vmem((tokens, LANES), F32),
        vmem((tokens, LANES), F32),
        vmem((tokens, LANES), F32),
        vmem((tokens, LANES), F32),
        vmem((protos, LANES), F32),
        vmem((1, protos), F32),
        vmem((ITERS, n_p, 2, tokens), F32),
        vmem((ITERS, n_z, 1, protos), F32),
        vmem((n_z, 2, tokens), F32),
        vmem((tokens, dim), F32),
        vmem((GROUP - 1, share, dim), F32),
        vmem((octets, share, dim), F32),
        vmem((tokens, dim), BF16),
        dma((ITERS, n_p - 1)), dma((ITERS, n_p - 1)),
        dma((ITERS, n_z - 1)), dma((ITERS, n_z - 1)),
        dma((n_z - 1,)), dma((n_z - 1,)),
        dma((n_z - 1,)), dma((n_z - 1,)),
        dma((n_z - 1, GROUP // 2 - 1)), dma((n_z - 1, GROUP // 2 - 1)),
        dma((n_z - 1,)), dma((n_z - 1,)),
        dma((GROUP - 1,)), dma((GROUP - 1,)),
        dma((one,)), dma((one,)),
        dma((GROUP - 1,)), dma((GROUP - 1,)),
    ]
    spec = pl.BlockSpec(memory_space=pltpu.VMEM)
    return pl.pallas_call(
        functools.partial(kernel, n_p, n_z),
        out_shape=(
            jax.ShapeDtypeStruct((patches, dim), BF16),
            jax.ShapeDtypeStruct((protos, dim), BF16),
        ),
        in_specs=[spec] * 6,
        out_specs=(spec, spec),
        scratch_shapes=scratch,
        compiler_params=pltpu.CompilerParams(
            collective_id=0, has_side_effects=True, vmem_limit_bytes=58 * 1024 * 1024
        ),
    )(sp, tp, positions.reshape(1, tokens), weight.reshape(1, tokens), pp, qp)


def solution(mesh):
    return jax.shard_map(
        functools.partial(body, mesh.shape["proto"], mesh.shape["batch"]),
        mesh=mesh,
        in_specs=(
            P("batch", None),
            P("batch", None),
            P("batch"),
            P("batch"),
            P("proto", None),
            P("proto", None),
        ),
        out_specs=(P("batch", None), P("proto", None)),
        check_vma=False,
    )
```

time: 270 us -> 68.1 us (0.25)
  waiting for transfers between devices: 127 us -> 0 us
  blocking collectives: 68.5 us -> 0 us
  Pallas kernels: 0 us -> 62.3 us
  other arithmetic: 38.5 us -> 0 us
  between operations: 14.3 us -> 0.66 us
  matrix products: 13.3 us -> 0 us
    psum x2 -> x0, waiting for transfers between devices: 127 us -> none  [the longest x1 79 us: body(): proto_total = lax.psum(proto_term, 'batch')]
    psum x6 -> x0, blocking collectives: 68.5 us -> none  [the longest x3 35.6 us: body(): lax.psum(jnp.sum(teacher_assignments * col_scale[None, :], axis=1), 'proto')]
    pallas_call x0 -> x1, Pallas kernels: none -> 62.3 us  [body(): pl.pallas_call(functools.partial(kernel, n_p, n_z), out_shape=(jax.ShapeD...]
    reduce_sum x10 -> x0, other arithmetic: 21.9 us -> none  [the longest x3 8.73 us: body(): jnp.sum(teacher_assignments * col_scale[None, :], axis=1)]
    dot_general x4 -> x0, matrix products: 13.3 us -> none  [the longest x2 7.17 us: exponentiated_similarity(): lax.dot_general(front_segment, rear_segment, (((1,), (1,)), ((), ())), pr...]
    scatter x1 -> x0, other arithmetic: 7.9 us -> none  [body(): patch_grad = jnp.zeros((patch_count, feature_grad.shape[1]), jnp.bfloat16...]
    convert_element_type x2 -> x0, other arithmetic: 7.77 us -> none  [the longest x1 5.05 us: body(): (token_weight[:, None] * (probability - target) / TEMP_STUDENT).astype(jn...]
    gather x2 -> x0, local copies, waits for them, and re-layouts: 5.54 us -> none  [the longest x1 2.77 us: body(): jnp.take(student_patches, local_rows, axis=0)]
  transfers between devices with their start and end apart: 2 -> 0, of which waited for: 2 -> 0; matrix products, arithmetic and copies ran while one was open for 5% -> 0% of each run, Pallas kernels for 0% -> 0%
where the time goes in v1:
time: 68.1 us; the launch traced here: 67.9 us
  Pallas kernels  62.3 us (91%)
  local copies, waits for them, and re-layouts  4.88 us (7%)
    pallas_call x1, Pallas kernels, body(): pl.pallas_call(functools.partial(kernel, n_p, n_z), out_shape=(jax.ShapeD...  62.3 us
    unnamed x6, local copies, waits for them, and re-layouts  3.03 us

profile of v1, /device:TPU:0, one launch (start us, length us, event | category | flops | bytes accessed | tf_op | source)
XLA Modules:
  0.0 67.9 jit_solution(10483982868528259111)
XLA Ops:
  0.6 0.0 copy-start.1
  0.6 1.3 %reshape.10.pos = s32[1,640]{1,0:T(1,128)} reshape(s32[640]{0:T(1024)} %param.8) | data formatting | bytes 5120 | tf_op jit(solution)/shard_map/reshape | solution.py:390
  1.9 0.0 copy-done.1
  1.9 0.6 reshape.11.weight
  2.5 62.3 %shard_map.77 = (bf16[1280,256]{1,0:T(8,128)(2,1)}, bf16[2048,256]{1,0:T(8,128)(2,1)}) custom-call(bf16[1280,256]{1,0:T(8,128)(2,1)} %sp.1, bf16[1280,256]{1,0:T(8,128)(2,1)} %tp.1, s32[1,640]{1,0:T(1,128)} %reshape.10.pos, f32[1,640]{1,0:T(1,128)} %reshape.11.weight, bf16[2048,256]{1,0:T(8,128)(2,1)} %pp.1, bf16[2048,256]{1,0:T(8,128)(2,1)} %qp.1), custom_call_target="tpu_custom_call" | custom-call | tf_op jit(solution)/shard_map/pallas_call | solution.py:378
  64.8 0.0 copy-start
  64.8 2.1 %copy.10 = bf16[1280,256]{1,0:T(8,128)(2,1)} copy(bf16[1280,256]{1,0:T(8,128)(2,1)} %get-tuple-element.4) | data formatting | bytes 1310720
  66.9 0.0 copy-done
  66.9 1.0 %copy.11 = bf16[2048,256]{1,0:T(8,128)(2,1)} copy(bf16[2048,256]{1,0:T(8,128)(2,1)S(1)} %copy-done) | data formatting | bytes 2097152
Async XLA Ops:
  0.6 1.3 %copy-start.1 = (f32[640]{0:T(1024)S(1)}, f32[640]{0:T(1024)}, u32[]{:S(2)}) copy-start(f32[640]{0:T(1024)} %param.9) | copy-start | bytes 7684
  64.8 2.1 %copy-start = (bf16[2048,256]{1,0:T(8,128)(2,1)S(1)}, bf16[2048,256]{1,0:T(8,128)(2,1)}, u32[]{:S(2)}) copy-start(bf16[2048,256]{1,0:T(8,128)(2,1)} %get-tuple-element.5) | copy-start | bytes 3145732

commit v2 on v1

--- a/solution.py
+++ b/solution.py
@@ -17,6 +17,7 @@
 STUDENT_RATE = LOG2E / TEMP_STUDENT
 GROUP = 8
 TILE = 256
+WIDE = 512
 LANES = 128
 MESH = pl.DeviceIdType.MESH
 F32 = jnp.float32
@@ -43,14 +44,14 @@
     n_p, n_z,
     sp, tp, pos, weight, pp, qp,
     patch_out, proto_out,
-    hot, tok, s_unit, s_norm, ph, qh, e_ref, s_ref, acc_ref, acc2_ref,
+    hot, hot_t, tok_s, tok_t, s_unit, s_norm, ph, qh, e_ref, s_ref, acc_ref, acc2_ref,
     rb_ref, ab_ref, cb_ref, crow_ref,
-    row_buf, col_buf, fac_buf, feat, rs_buf, rs2_buf, fgrad,
+    row_buf, col_buf, fac_buf, feat, pair_buf, rs_buf, rs2_buf, fgrad,
     row_send, row_recv, col_send, col_recv, fac_send, fac_recv,
     t1_send, t1_recv, t2_send, t2_recv, t3_send, t3_recv,
-    rs_send, rs_recv, rs2_send, rs2_recv, ag_send, ag_recv,
+    pair_send, pair_recv, rs_send, rs_recv, rs2_send, rs2_recv, ag_send, ag_recv,
 ):
-    tokens = tok.shape[1]
+    tokens = tok_s.shape[1]
     patches, dim = sp.shape
     protos = pp.shape[0]
     share = tokens // GROUP
@@ -97,7 +98,7 @@
         for copy in copies:
             copy.wait()
 
-    local = pos[...] - me_z * patches
+    local = pos[...].reshape(1, tokens) - me_z * patches
     local_col = as_columns(local.astype(F32))
     lane = lax.broadcasted_iota(jnp.int32, (tokens, LANES), 1).astype(F32)
     for t in range(patches // LANES):
@@ -105,7 +106,7 @@
             local_col == lane + float(t * LANES), 1.0, 0.0
         ).astype(BF16)
 
-    @pl.loop(0, tokens // LANES)
+    @pl.loop(0, tokens // LANES, unroll=True)
     def _(i):
         rows = pl.ds(pl.multiple_of(i * LANES, LANES), LANES)
         picked = hot[rows, :]
@@ -115,16 +116,16 @@
         s_unit[rows, :] = unit
         s_norm[rows, :] = jnp.broadcast_to(norm, (LANES, LANES))
         teacher = dot_nn(picked, tp[...])
-        tok[me_z, rows, 0:dim] = unit.astype(BF16)
-        tok[me_z, rows, dim:2 * dim] = (teacher / row_norm(teacher)).astype(BF16)
-
-    @pl.loop(0, protos // TILE)
+        tok_s[me_z, rows, :] = unit.astype(BF16)
+        tok_t[me_z, rows, :] = (teacher / row_norm(teacher)).astype(BF16)
+
+    @pl.loop(0, protos // TILE, unroll=4)
     def _(i):
         rows = pl.ds(pl.multiple_of(i * TILE, TILE), TILE)
         values = qp[rows, :].astype(F32)
         half = (values / row_norm(values)).astype(BF16)
         qh[rows, :] = half
-        exps = jnp.exp2(dot_nt(tok[me_z, :, dim:2 * dim], half) * TEACHER_RATE)
+        exps = jnp.exp2(dot_nt(tok_t[me_z], half) * TEACHER_RATE)
         e_ref[:, rows] = exps
         col_buf[0, me_z, :, rows] = jnp.sum(exps, axis=0, keepdims=True)
 
@@ -134,37 +135,37 @@
 
     acc2_ref[...] = jnp.zeros_like(acc2_ref)
 
-    @pl.loop(0, protos // TILE)
+    @pl.loop(0, protos // TILE, unroll=4)
     def _(i):
         rows = pl.ds(pl.multiple_of(i * TILE, TILE), TILE)
         values = pp[rows, :].astype(F32)
         half = (values / row_norm(values)).astype(BF16)
         ph[rows, :] = half
-        exps = jnp.exp2(dot_nt(tok[me_z, :, 0:dim], half) * STUDENT_RATE)
+        exps = jnp.exp2(dot_nt(tok_s[me_z], half) * STUDENT_RATE)
         s_ref[:, rows] = exps
         acc2_ref[...] += exps[:, 0:LANES] + exps[:, LANES:2 * LANES]
 
     def lane_sums(ref):
         return jnp.sum(jnp.transpose(ref[...]), axis=0, keepdims=True)
 
-    t1 = []
-    for j in range(1, n_z):
-        block = tok.at[me_z, pl.ds(rows_of(g), share), :]
-        t1.append(remote(block, block, t1_send.at[j - 1], t1_recv.at[j - 1], me_p, (me_z + j) % n_z))
-    t2 = []
-    t3 = []
     other = me_p + 1 - 2 * (me_p % 2)
-    for j in range(1, n_z):
-        source = (me_z + n_z - j) % n_z
-        block = tok.at[source, pl.ds(rows_of(g), share), :]
-        for k in range(1, GROUP // 2):
-            t2.append(remote(
-                block, block, t2_send.at[j - 1, k - 1], t2_recv.at[j - 1, k - 1],
-                octet * GROUP + (g + 2 * k) % GROUP, me_z,
+    half_rows = pl.ds(pl.multiple_of((g % 2) * (tokens // 2), 16), tokens // 2)
+    t1, t2, t3 = ([], []), ([], []), ([], [])
+    for h, tok in enumerate((tok_t, tok_s)):
+        for j in range(1, n_z):
+            block = tok.at[me_z, pl.ds(rows_of(g), share), :]
+            t1[h].append(remote(
+                block, block, t1_send.at[h, j - 1], t1_recv.at[h, j - 1], me_p, (me_z + j) % n_z,
             ))
-        half_rows = pl.ds(pl.multiple_of((g % 2) * (tokens // 2), 16), tokens // 2)
-        block = tok.at[source, half_rows, :]
-        t3.append(remote(block, block, t3_send.at[j - 1], t3_recv.at[j - 1], other, me_z))
+            source = (me_z + n_z - j) % n_z
+            block = tok.at[source, pl.ds(rows_of(g), share), :]
+            for k in range(1, GROUP // 2):
+                t2[h].append(remote(
+                    block, block, t2_send.at[h, j - 1, k - 1], t2_recv.at[h, j - 1, k - 1],
+                    octet * GROUP + (g + 2 * k) % GROUP, me_z,
+                ))
+            block = tok.at[source, half_rows, :]
+            t3[h].append(remote(block, block, t3_send.at[h, j - 1], t3_recv.at[h, j - 1], other, me_z))
 
     row_scale = jnp.ones((1, tokens), F32)
     student_total = None
@@ -186,15 +187,21 @@
                 col_buf[it, me_z, :, t * LANES:(t + 1) * LANES] = jnp.sum(sums[t], axis=0, keepdims=True)
             copies = col_copies(it)
             start(copies)
+        if it == 1:
+            index = lax.broadcasted_iota(jnp.int32, (LANES, tokens), 0)
+            for t in range(patches // LANES):
+                hot_t[t * LANES:(t + 1) * LANES, :] = jnp.where(
+                    index + t * LANES == local, 1.0, 0.0
+                ).astype(BF16)
         wait(copies)
-        if it == 0:
-            start(t1)
+        if it < 2:
+            start(t1[it])
         total = col_buf[it, 0]
         for q in range(1, n_z):
             total = total + col_buf[it, q]
         crow_ref[...] = 1.0 / total
 
-        @pl.loop(0, tokens // 64)
+        @pl.loop(0, tokens // 64, unroll=2)
         def _(i):
             rows = pl.ds(pl.multiple_of(i * 64, 64), 64)
             running = e_ref[rows, 0:LANES] * crow_ref[:, 0:LANES]
@@ -211,8 +218,11 @@
             cb_ref[...] = as_columns(crow_ref[...])
         wait(copies)
         if it == 1:
-            wait(t1)
-            start(t2)
+            wait(t2[0])
+            start(t3[0])
+        if it < 2:
+            wait(t1[it])
+            start(t2[it])
         total = row_buf[it, 0]
         for q in range(1, n_p):
             total = total + row_buf[it, q]
@@ -221,7 +231,7 @@
         if it < ITERS - 1:
             rb_ref[...] = as_columns(row_scale)
 
-    gain = weight[...] / TEMP_STUDENT
+    gain = weight[...].reshape(1, tokens) / TEMP_STUDENT
     student_gain = gain / student_total
     teacher_gain = gain * row_scale
     fac_buf[me_z, 0:1, :] = student_gain
@@ -232,15 +242,14 @@
         for j in range(1, n_z)
     ]
     start(fac)
-    wait(t2)
-    start(t3)
+    wait(t2[1])
+    start(t3[1])
 
     rb_ref[...] = as_columns(teacher_gain)
     ab_ref[...] = as_columns(student_gain)
 
-    @pl.loop(0, tokens // LANES)
-    def _(i):
-        rows = pl.ds(pl.multiple_of(i * LANES, LANES), LANES)
+    def feature_rows(first, count):
+        rows = pl.ds(pl.multiple_of(first, 16), count)
         a = ab_ref[rows, :]
         b = rb_ref[rows, :]
         parts = []
@@ -250,32 +259,36 @@
                 (s_ref[rows, cols] * a - e_ref[rows, cols] * b * crow_ref[:, cols]).astype(BF16)
             )
         feat[rows, :] = dot_nn(jnp.concatenate(parts, axis=1), ph[...])
-
-    rs = []
-    for j in range(1, GROUP):
-        to = (g + j) % GROUP
-        rs.append(remote(
-            feat.at[pl.ds(rows_of(to), share), :], rs_buf.at[j - 1],
-            rs_send.at[j - 1], rs_recv.at[j - 1], octet * GROUP + to, me_z,
+        return rows
+
+    quarter = tokens // 4
+    theirs = ((g + 1) % 2) * (tokens // 2)
+    ours = (g % 2) * (tokens // 2)
+    pair = []
+    for i in range(2):
+        rows = feature_rows(theirs + i * quarter, quarter)
+        pair.append(remote(
+            feat.at[rows, :], pair_buf.at[i], pair_send.at[i], pair_recv.at[i], other, me_z,
         ))
-    start(rs)
-    wait(fac)
-    wait(t3)
+        start(pair[i:])
+    for i in range(2):
+        feature_rows(ours + i * quarter, quarter)
+
 
     def proto_tile(i):
-        rows = pl.ds(pl.multiple_of(i * TILE, TILE), TILE)
+        rows = pl.ds(pl.multiple_of(i * WIDE, WIDE), WIDE)
         p_half = ph[rows, :]
         q_half = qh[rows, :]
         c = jnp.concatenate([cb_ref[rows, :]] * (tokens // LANES), axis=1)
 
         def block(z, running):
-            student = tok[z, :, 0:dim]
+            student = tok_s[z]
             prob = jnp.exp2(dot_nt(p_half, student) * STUDENT_RATE)
-            target = jnp.exp2(dot_nt(q_half, tok[z, :, dim:2 * dim]) * TEACHER_RATE)
+            target = jnp.exp2(dot_nt(q_half, tok_t[z]) * TEACHER_RATE)
             coefficient = prob * fac_buf[z, 0:1, :] - target * fac_buf[z, 1:2, :] * c
             return running + dot_nn(coefficient.astype(BF16), student)
 
-        total = jnp.zeros((TILE, dim), F32)
+        total = jnp.zeros((WIDE, dim), F32)
         if n_z <= 4:
             for z in range(n_z):
                 total = block(z, total)
@@ -287,14 +300,29 @@
         inner = jnp.sum(total * unit, axis=1, keepdims=True)
         proto_out[rows, :] = ((total - inner * unit) / norm).astype(BF16)
 
-    tiles = protos // TILE
-    early = tiles - 3
+    tiles = protos // WIDE
+    wait(pair)
+    for i in range(2):
+        rows = pl.ds(pl.multiple_of(ours + i * quarter, 16), quarter)
+        feat[rows, :] += pair_buf[i]
+    rs = []
+    for j in range(1, GROUP // 2):
+        to = (g + 2 * j) % GROUP
+        rs.append(remote(
+            feat.at[pl.ds(rows_of(to), share), :], rs_buf.at[j - 1],
+            rs_send.at[j - 1], rs_recv.at[j - 1], octet * GROUP + to, me_z,
+        ))
+    start(rs)
+    wait(fac)
+    wait(t3[0])
+    wait(t3[1])
+    early = tiles // 2
     pl.loop(0, early)(proto_tile)
 
     wait(rs)
     own = pl.ds(rows_of(g), share)
     total = feat[own, :]
-    for j in range(1, GROUP):
+    for j in range(1, GROUP // 2):
         total = total + rs_buf[j - 1]
     if octets > 1:
         rs2_buf[octet] = total
@@ -328,9 +356,7 @@
     @pl.loop(0, patches // TILE)
     def _(i):
         rows = pl.ds(pl.multiple_of(i * TILE, TILE), TILE)
-        index = lax.broadcasted_iota(jnp.int32, (TILE, tokens), 0) + i * TILE
-        chosen = jnp.where(index == local, 1.0, 0.0).astype(BF16)
-        patch_out[rows, :] = dot_nn(chosen, fgrad[...]).astype(BF16)
+        patch_out[rows, :] = dot_nn(hot_t[rows, :], fgrad[...]).astype(BF16)
 
 
 def body(n_p, n_z, sp, tp, positions, weight, pp, qp):
@@ -344,7 +370,9 @@
     one = max(octets - 1, 1)
     scratch = [
         vmem((tokens, patches), BF16),
-        vmem((n_z, tokens, 2 * dim), BF16),
+        vmem((patches, tokens), BF16),
+        vmem((n_z, tokens, dim), BF16),
+        vmem((n_z, tokens, dim), BF16),
         vmem((tokens, dim), F32),
         vmem((tokens, LANES), F32),
         vmem((protos, dim), BF16),
@@ -361,16 +389,18 @@
         vmem((ITERS, n_z, 1, protos), F32),
         vmem((n_z, 2, tokens), F32),
         vmem((tokens, dim), F32),
-        vmem((GROUP - 1, share, dim), F32),
+        vmem((2, tokens // 4, dim), F32),
+        vmem((GROUP // 2 - 1, share, dim), F32),
         vmem((octets, share, dim), F32),
         vmem((tokens, dim), BF16),
         dma((ITERS, n_p - 1)), dma((ITERS, n_p - 1)),
         dma((ITERS, n_z - 1)), dma((ITERS, n_z - 1)),
         dma((n_z - 1,)), dma((n_z - 1,)),
-        dma((n_z - 1,)), dma((n_z - 1,)),
-        dma((n_z - 1, GROUP // 2 - 1)), dma((n_z - 1, GROUP // 2 - 1)),
-        dma((n_z - 1,)), dma((n_z - 1,)),
-        dma((GROUP - 1,)), dma((GROUP - 1,)),
+        dma((2, n_z - 1)), dma((2, n_z - 1)),
+        dma((2, n_z - 1, GROUP // 2 - 1)), dma((2, n_z - 1, GROUP // 2 - 1)),
+        dma((2, n_z - 1)), dma((2, n_z - 1)),
+        dma((2,)), dma((2,)),
+        dma((GROUP // 2 - 1,)), dma((GROUP // 2 - 1,)),
         dma((one,)), dma((one,)),
         dma((GROUP - 1,)), dma((GROUP - 1,)),
     ]
@@ -387,7 +417,7 @@
         compiler_params=pltpu.CompilerParams(
             collective_id=0, has_side_effects=True, vmem_limit_bytes=58 * 1024 * 1024
         ),
-    )(sp, tp, positions.reshape(1, tokens), weight.reshape(1, tokens), pp, qp)
+    )(sp, tp, positions, weight, pp, qp)
 
 
 def solution(mesh):

time: 68.1 us -> 57.4 us (0.84)
  Pallas kernels: 62.3 us -> 53.6 us
  local copies, waits for them, and re-layouts: 4.88 us -> 3.03 us
    pallas_call x1, Pallas kernels: 62.3 us -> 53.6 us  [body(): pl.pallas_call(functools.partial(kernel, n_p, n_z), out_shape=(jax.ShapeD...]
    reshape x2 -> x0, local copies, waits for them, and re-layouts: 1.85 us -> none  [the longest x1 1.27 us: body(): positions.reshape(1, tokens)]
    unnamed x6 -> x4, local copies, waits for them, and re-layouts: 3.03 us -> 3.03 us
where the time goes in v2:
time: 57.4 us; the launch traced here: 57.3 us
  Pallas kernels  53.6 us (93%)
  local copies, waits for them, and re-layouts  3.03 us (5%)
  between operations  0.65 us (1%)
    pallas_call x1, Pallas kernels, body(): pl.pallas_call(functools.partial(kernel, n_p, n_z), out_shape=(jax.ShapeD...  53.6 us
    unnamed x4, local copies, waits for them, and re-layouts  3.03 us

profile of v2, /device:TPU:0, one launch (start us, length us, event | category | flops | bytes accessed | tf_op | source)
XLA Modules:
  0.0 57.3 jit_solution(684789289971876567)
XLA Ops:
  0.6 53.6 %shard_map.77 = (bf16[1280,256]{1,0:T(8,128)(2,1)}, bf16[2048,256]{1,0:T(8,128)(2,1)}) custom-call(bf16[1280,256]{1,0:T(8,128)(2,1)} %sp.1, bf16[1280,256]{1,0:T(8,128)(2,1)} %tp.1, s32[640]{0:T(1024)} %pos.1, f32[640]{0:T(1024)} %weight.1, bf16[2048,256]{1,0:T(8,128)(2,1)} %pp.1, bf16[2048,256]{1,0:T(8,128)(2,1)} %qp.1), custom_call_target="tpu_custom_call" | custom-call | tf_op jit(solution)/shard_map/pallas_call | solution.py:408
  54.2 0.0 copy-start
  54.3 2.1 %copy.10 = bf16[1280,256]{1,0:T(8,128)(2,1)} copy(bf16[1280,256]{1,0:T(8,128)(2,1)} %get-tuple-element.4) | data formatting | bytes 1310720
  56.3 0.0 copy-done
  56.3 1.0 %copy.11 = bf16[2048,256]{1,0:T(8,128)(2,1)} copy(bf16[2048,256]{1,0:T(8,128)(2,1)S(1)} %copy-done) | data formatting | bytes 2097152
Async XLA Ops:
  54.2 2.1 %copy-start = (bf16[2048,256]{1,0:T(8,128)(2,1)S(1)}, bf16[2048,256]{1,0:T(8,128)(2,1)}, u32[]{:S(2)}) copy-start(bf16[2048,256]{1,0:T(8,128)(2,1)} %get-tuple-element.5) | copy-start | bytes 3145732

commit v3 on v2

--- a/solution.py
+++ b/solution.py
@@ -17,7 +17,8 @@
 STUDENT_RATE = LOG2E / TEMP_STUDENT
 GROUP = 8
 TILE = 256
-WIDE = 512
+WIDE = 1024
+CHUNK = 512
 LANES = 128
 MESH = pl.DeviceIdType.MESH
 F32 = jnp.float32
@@ -42,16 +43,16 @@
 
 def kernel(
     n_p, n_z,
-    sp, tp, pos, weight, pp, qp,
+    sp, tp, pos, weight, pp_in, qp_in,
     patch_out, proto_out,
-    hot, hot_t, tok_s, tok_t, s_unit, s_norm, ph, qh, e_ref, s_ref, acc_ref, acc2_ref,
+    pp, qp, load_sem, hot, hot_t, tok_s, tok_t, fac_flat, s_unit, s_norm, ph, qh, e_ref, s_ref, acc_ref, acc2_ref,
     rb_ref, ab_ref, cb_ref, crow_ref,
     row_buf, col_buf, fac_buf, feat, pair_buf, rs_buf, rs2_buf, fgrad,
     row_send, row_recv, col_send, col_recv, fac_send, fac_recv,
     t1_send, t1_recv, t2_send, t2_recv, t3_send, t3_recv,
     pair_send, pair_recv, rs_send, rs_recv, rs2_send, rs2_recv, ag_send, ag_recv,
 ):
-    tokens = tok_s.shape[1]
+    tokens = pos.shape[0]
     patches, dim = sp.shape
     protos = pp.shape[0]
     share = tokens // GROUP
@@ -61,9 +62,18 @@
     octet = me_p // GROUP
     g = me_p % GROUP
 
+    def block_rows(z, first, count):
+        return pl.ds(pl.multiple_of(z * tokens + first, 16), count)
+
     def rows_of(member):
         return pl.multiple_of(((member % 2) * (GROUP // 2) + member // 2) * share, 16)
 
+    loads = [
+        pltpu.make_async_copy(qp_in, qp, load_sem.at[0]),
+        pltpu.make_async_copy(pp_in, pp, load_sem.at[1]),
+    ]
+    for load in loads:
+        load.start()
     barrier = pltpu.get_barrier_semaphore()
     for j in range(1, n_p):
         pl.semaphore_signal(barrier, inc=1, device_id=((me_p + j) % n_p, me_z), device_id_type=MESH)
@@ -94,9 +104,12 @@
         for copy in copies:
             copy.start()
 
+    pending = []
+
     def wait(copies):
         for copy in copies:
-            copy.wait()
+            copy.wait_recv()
+        pending.extend(copies)
 
     local = pos[...].reshape(1, tokens) - me_z * patches
     local_col = as_columns(local.astype(F32))
@@ -116,8 +129,10 @@
         s_unit[rows, :] = unit
         s_norm[rows, :] = jnp.broadcast_to(norm, (LANES, LANES))
         teacher = dot_nn(picked, tp[...])
-        tok_s[me_z, rows, :] = unit.astype(BF16)
-        tok_t[me_z, rows, :] = (teacher / row_norm(teacher)).astype(BF16)
+        tok_s[block_rows(me_z, i * LANES, LANES), :] = unit.astype(BF16)
+        tok_t[block_rows(me_z, i * LANES, LANES), :] = (teacher / row_norm(teacher)).astype(BF16)
+
+    loads[0].wait()
 
     @pl.loop(0, protos // TILE, unroll=4)
     def _(i):
@@ -125,7 +140,7 @@
         values = qp[rows, :].astype(F32)
         half = (values / row_norm(values)).astype(BF16)
         qh[rows, :] = half
-        exps = jnp.exp2(dot_nt(tok_t[me_z], half) * TEACHER_RATE)
+        exps = jnp.exp2(dot_nt(tok_t[block_rows(me_z, 0, tokens), :], half) * TEACHER_RATE)
         e_ref[:, rows] = exps
         col_buf[0, me_z, :, rows] = jnp.sum(exps, axis=0, keepdims=True)
 
@@ -134,6 +149,7 @@
     start(copies)
 
     acc2_ref[...] = jnp.zeros_like(acc2_ref)
+    loads[1].wait()
 
     @pl.loop(0, protos // TILE, unroll=4)
     def _(i):
@@ -141,7 +157,7 @@
         values = pp[rows, :].astype(F32)
         half = (values / row_norm(values)).astype(BF16)
         ph[rows, :] = half
-        exps = jnp.exp2(dot_nt(tok_s[me_z], half) * STUDENT_RATE)
+        exps = jnp.exp2(dot_nt(tok_s[block_rows(me_z, 0, tokens), :], half) * STUDENT_RATE)
         s_ref[:, rows] = exps
         acc2_ref[...] += exps[:, 0:LANES] + exps[:, LANES:2 * LANES]
 
@@ -149,22 +165,21 @@
         return jnp.sum(jnp.transpose(ref[...]), axis=0, keepdims=True)
 
     other = me_p + 1 - 2 * (me_p % 2)
-    half_rows = pl.ds(pl.multiple_of((g % 2) * (tokens // 2), 16), tokens // 2)
     t1, t2, t3 = ([], []), ([], []), ([], [])
     for h, tok in enumerate((tok_t, tok_s)):
         for j in range(1, n_z):
-            block = tok.at[me_z, pl.ds(rows_of(g), share), :]
+            block = tok.at[block_rows(me_z, rows_of(g), share), :]
             t1[h].append(remote(
                 block, block, t1_send.at[h, j - 1], t1_recv.at[h, j - 1], me_p, (me_z + j) % n_z,
             ))
             source = (me_z + n_z - j) % n_z
-            block = tok.at[source, pl.ds(rows_of(g), share), :]
+            block = tok.at[block_rows(source, rows_of(g), share), :]
             for k in range(1, GROUP // 2):
                 t2[h].append(remote(
                     block, block, t2_send.at[h, j - 1, k - 1], t2_recv.at[h, j - 1, k - 1],
                     octet * GROUP + (g + 2 * k) % GROUP, me_z,
                 ))
-            block = tok.at[source, half_rows, :]
+            block = tok.at[block_rows(source, (g % 2) * (tokens // 2), tokens // 2), :]
             t3[h].append(remote(block, block, t3_send.at[h, j - 1], t3_recv.at[h, j - 1], other, me_z))
 
     row_scale = jnp.ones((1, tokens), F32)
@@ -279,21 +294,23 @@
         rows = pl.ds(pl.multiple_of(i * WIDE, WIDE), WIDE)
         p_half = ph[rows, :]
         q_half = qh[rows, :]
-        c = jnp.concatenate([cb_ref[rows, :]] * (tokens // LANES), axis=1)
-
-        def block(z, running):
-            student = tok_s[z]
+        c = jnp.concatenate([cb_ref[rows, :]] * (CHUNK // LANES), axis=1)
+
+        def block(k, running):
+            part = pl.ds(pl.multiple_of(k * CHUNK, CHUNK), CHUNK)
+            student = tok_s[part, :]
             prob = jnp.exp2(dot_nt(p_half, student) * STUDENT_RATE)
-            target = jnp.exp2(dot_nt(q_half, tok_t[z]) * TEACHER_RATE)
-            coefficient = prob * fac_buf[z, 0:1, :] - target * fac_buf[z, 1:2, :] * c
+            target = jnp.exp2(dot_nt(q_half, tok_t[part, :]) * TEACHER_RATE)
+            coefficient = prob * fac_flat[0:1, part] - target * fac_flat[1:2, part] * c
             return running + dot_nn(coefficient.astype(BF16), student)
 
         total = jnp.zeros((WIDE, dim), F32)
-        if n_z <= 4:
-            for z in range(n_z):
-                total = block(z, total)
+        chunks = n_z * tokens // CHUNK
+        if chunks <= 5:
+            for k in range(chunks):
+                total = block(k, total)
         else:
-            total = lax.fori_loop(0, n_z, block, total)
+            total = lax.fori_loop(0, chunks, block, total)
         values = pp[rows, :].astype(F32)
         norm = row_norm(values)
         unit = values / norm
@@ -316,6 +333,8 @@
     wait(fac)
     wait(t3[0])
     wait(t3[1])
+    for z in range(n_z):
+        fac_flat[:, z * tokens:(z + 1) * tokens] = fac_buf[z]
     early = tiles // 2
     pl.loop(0, early)(proto_tile)
 
@@ -352,6 +371,8 @@
     pl.loop(early, tiles)(proto_tile)
 
     wait(ag)
+    for copy in pending:
+        copy.wait_send()
 
     @pl.loop(0, patches // TILE)
     def _(i):
@@ -369,10 +390,14 @@
     dma = pltpu.SemaphoreType.DMA
     one = max(octets - 1, 1)
     scratch = [
+        vmem((protos, dim), BF16),
+        vmem((protos, dim), BF16),
+        dma((2,)),
         vmem((tokens, patches), BF16),
         vmem((patches, tokens), BF16),
-        vmem((n_z, tokens, dim), BF16),
-        vmem((n_z, tokens, dim), BF16),
+        vmem((n_z * tokens, dim), BF16),
+        vmem((n_z * tokens, dim), BF16),
+        vmem((2, n_z * tokens), F32),
         vmem((tokens, dim), F32),
         vmem((tokens, LANES), F32),
         vmem((protos, dim), BF16),
@@ -411,7 +436,7 @@
             jax.ShapeDtypeStruct((patches, dim), BF16),
             jax.ShapeDtypeStruct((protos, dim), BF16),
         ),
-        in_specs=[spec] * 6,
+        in_specs=[spec] * 4 + [pl.BlockSpec(memory_space=pl.ANY)] * 2,
         out_specs=(spec, spec),
         scratch_shapes=scratch,
         compiler_params=pltpu.CompilerParams(

time: 57.4 us -> 55.1 us (0.960)
  Pallas kernels: 53.6 us -> 51.3 us
    pallas_call x1, Pallas kernels: 53.6 us -> 51.3 us  [body(): pl.pallas_call(functools.partial(kernel, n_p, n_z), out_shape=(jax.ShapeD...]
where the time goes in v3:
time: 55.1 us; the launch traced here: 54.9 us
  Pallas kernels  51.3 us (93%)
  local copies, waits for them, and re-layouts  3.03 us (5%)
  between operations  0.65 us (1%)
    pallas_call x1, Pallas kernels, body(): pl.pallas_call(functools.partial(kernel, n_p, n_z), out_shape=(jax.ShapeD...  51.3 us
    unnamed x4, local copies, waits for them, and re-layouts  3.03 us

profile of v3, /device:TPU:0, one launch (start us, length us, event | category | flops | bytes accessed | tf_op | source)
XLA Modules:
  0.0 54.9 jit_solution(6351153824599380230)
XLA Ops:
  0.6 51.3 %shard_map.77 = (bf16[1280,256]{1,0:T(8,128)(2,1)}, bf16[2048,256]{1,0:T(8,128)(2,1)}) custom-call(bf16[1280,256]{1,0:T(8,128)(2,1)} %sp.1, bf16[1280,256]{1,0:T(8,128)(2,1)} %tp.1, s32[640]{0:T(1024)} %pos.1, f32[640]{0:T(1024)} %weight.1, bf16[2048,256]{1,0:T(8,128)(2,1)} %pp_in.1, bf16[2048,256]{1,0:T(8,128)(2,1)} %qp_in.1), custom_call_target="tpu_custom_call" | custom-call | tf_op jit(solution)/shard_map/pallas_call | solution.py:433
  51.9 0.0 copy-start
  51.9 2.1 %copy.10 = bf16[1280,256]{1,0:T(8,128)(2,1)} copy(bf16[1280,256]{1,0:T(8,128)(2,1)} %get-tuple-element.4) | data formatting | bytes 1310720
  54.0 0.0 copy-done
  54.0 1.0 %copy.11 = bf16[2048,256]{1,0:T(8,128)(2,1)} copy(bf16[2048,256]{1,0:T(8,128)(2,1)S(1)} %copy-done) | data formatting | bytes 2097152
Async XLA Ops:
  51.9 2.1 %copy-start = (bf16[2048,256]{1,0:T(8,128)(2,1)S(1)}, bf16[2048,256]{1,0:T(8,128)(2,1)}, u32[]{:S(2)}) copy-start(bf16[2048,256]{1,0:T(8,128)(2,1)} %get-tuple-element.5) | copy-start | bytes 3145732

commit v4 on v3

--- a/solution.py
+++ b/solution.py
@@ -184,6 +184,7 @@
 
     row_scale = jnp.ones((1, tokens), F32)
     student_total = None
+    student_row = lane_sums(acc2_ref)
     for it in range(ITERS):
         if it > 0:
             def col_step(i, carry):
@@ -197,6 +198,7 @@
             sums = lax.fori_loop(
                 0, tokens // 32, col_step,
                 tuple(jnp.zeros((8, LANES), F32) for _ in range(protos // LANES)),
+                unroll=2,
             )
             for t in range(protos // LANES):
                 col_buf[it, me_z, :, t * LANES:(t + 1) * LANES] = jnp.sum(sums[t], axis=0, keepdims=True)
@@ -226,7 +228,7 @@
             acc_ref[rows, :] = running
 
         row_buf[it, me_p, 0:1, :] = lane_sums(acc_ref)
-        row_buf[it, me_p, 1:2, :] = lane_sums(acc2_ref)
+        row_buf[it, me_p, 1:2, :] = student_row
         copies = row_copies(it)
         start(copies)
         if it == ITERS - 1:
@@ -242,7 +244,8 @@
         for q in range(1, n_p):
             total = total + row_buf[it, q]
         row_scale = row_scale / (row_scale * total[0:1, :])
-        student_total = total[1:2, :]
+        if it == 0:
+            student_total = total[1:2, :]
         if it < ITERS - 1:
             rb_ref[...] = as_columns(row_scale)
 
@@ -374,7 +377,7 @@
     for copy in pending:
         copy.wait_send()
 
-    @pl.loop(0, patches // TILE)
+    @pl.loop(0, patches // TILE, unroll=True)
     def _(i):
         rows = pl.ds(pl.multiple_of(i * TILE, TILE), TILE)
         patch_out[rows, :] = dot_nn(hot_t[rows, :], fgrad[...]).astype(BF16)

time: 55.1 us -> 54.5 us (0.989)
  Pallas kernels: 51.3 us -> 50.7 us
    pallas_call x1, Pallas kernels: 51.3 us -> 50.7 us  [body(): pl.pallas_call(functools.partial(kernel, n_p, n_z), out_shape=(jax.ShapeD...]
where the time goes in v4:
time: 54.5 us; the launch traced here: 54.4 us
  Pallas kernels  50.7 us (93%)
  local copies, waits for them, and re-layouts  3.03 us (6%)
  between operations  0.65 us (1%)
    pallas_call x1, Pallas kernels, body(): pl.pallas_call(functools.partial(kernel, n_p, n_z), out_shape=(jax.ShapeD...  50.7 us
    unnamed x4, local copies, waits for them, and re-layouts  3.03 us

profile of v4, /device:TPU:0, one launch (start us, length us, event | category | flops | bytes accessed | tf_op | source)
XLA Modules:
  0.0 54.4 jit_solution(16780994343724968200)
XLA Ops:
  0.6 50.7 %shard_map.77 = (bf16[1280,256]{1,0:T(8,128)(2,1)}, bf16[2048,256]{1,0:T(8,128)(2,1)}) custom-call(bf16[1280,256]{1,0:T(8,128)(2,1)} %sp.1, bf16[1280,256]{1,0:T(8,128)(2,1)} %tp.1, s32[640]{0:T(1024)} %pos.1, f32[640]{0:T(1024)} %weight.1, bf16[2048,256]{1,0:T(8,128)(2,1)} %pp_in.1, bf16[2048,256]{1,0:T(8,128)(2,1)} %qp_in.1), custom_call_target="tpu_custom_call" | custom-call | tf_op jit(solution)/shard_map/pallas_call | solution.py:436
  51.3 0.0 copy-start
  51.4 2.1 %copy.10 = bf16[1280,256]{1,0:T(8,128)(2,1)} copy(bf16[1280,256]{1,0:T(8,128)(2,1)} %get-tuple-element.4) | data formatting | bytes 1310720
  53.4 0.0 copy-done
  53.4 1.0 %copy.11 = bf16[2048,256]{1,0:T(8,128)(2,1)} copy(bf16[2048,256]{1,0:T(8,128)(2,1)S(1)} %copy-done) | data formatting | bytes 2097152
Async XLA Ops:
  51.3 2.1 %copy-start = (bf16[2048,256]{1,0:T(8,128)(2,1)S(1)}, bf16[2048,256]{1,0:T(8,128)(2,1)}, u32[]{:S(2)}) copy-start(bf16[2048,256]{1,0:T(8,128)(2,1)} %get-tuple-element.5) | copy-start | bytes 3145732
